TPU v7x, 32 devices: a whole 2x2x4 slice. The times are simulated.
32 devices in a mesh: fsdp: 32 (over z, y, x, core).
Axes of the slice: x: 2, y: 2, z: 4, core: 2. Of those that a mesh axis runs over, the one named last changes fastest.
Arguments:
- inputs: bfloat16 [2, 4096, 1280], P(None, 'fsdp'), may hold values from -6 to 6
- cotangent: bfloat16 [2, 4096, 1280], P(None, 'fsdp'), may hold values from -6 to 6
- lengths: int32 [2, 4], replicated, may hold values from 512 to 1024, as said below
- first_gain: float32 [1280], P('fsdp'), may hold values from 0.25 to 1.75
- first_shift: float32 [1280], P('fsdp'), may hold values from -3 to 3
- query_weight: float32 [1280, 1280], P('fsdp'), may hold values from -0.15625 to 0.15625
- query_bias: float32 [1280], P('fsdp'), may hold values from -3 to 3
- key_weight: float32 [1280, 1280], P('fsdp'), may hold values from -0.15625 to 0.15625
- value_weight: float32 [1280, 1280], P('fsdp'), may hold values from -0.15625 to 0.15625
- value_bias: float32 [1280], P('fsdp'), may hold values from -3 to 3
- output_weight: float32 [1280, 1280], P('fsdp'), may hold values from -1.25 to 1.25
- output_bias: float32 [1280], P('fsdp'), may hold values from -3 to 3
- second_gain: float32 [1280], P('fsdp'), may hold values from 0.25 to 1.75
- second_shift: float32 [1280], P('fsdp'), may hold values from -3 to 3
- expand_weight: float32 [1280, 5120], P('fsdp'), may hold values from -0.15625 to 0.15625
- expand_bias: float32 [5120], P('fsdp'), may hold values from -3 to 3
- shrink_weight: float32 [5120, 1280], P('fsdp'), may hold values from -0.078125 to 0.078125
- shrink_bias: float32 [1280], P('fsdp'), may hold values from -3 to 3
Outputs:
- block_out: bfloat16 [2, 4096, 1280], P(None, 'fsdp')
- input_grad: bfloat16 [2, 4096, 1280], P(None, 'fsdp')
- grad_first_gain: float32 [1280], P('fsdp')
- grad_first_shift: float32 [1280], P('fsdp')
- grad_query_weight: float32 [1280, 1280], P('fsdp')
- grad_query_bias: float32 [1280], P('fsdp')
- grad_key_weight: float32 [1280, 1280], P('fsdp')
- grad_value_weight: float32 [1280, 1280], P('fsdp')
- grad_value_bias: float32 [1280], P('fsdp')
- grad_output_weight: float32 [1280, 1280], P('fsdp')
- grad_output_bias: float32 [1280], P('fsdp')
- grad_second_gain: float32 [1280], P('fsdp')
- grad_second_shift: float32 [1280], P('fsdp')
- grad_expand_weight: float32 [1280, 5120], P('fsdp')
- grad_expand_bias: float32 [5120], P('fsdp')
- grad_shrink_weight: float32 [5120, 1280], P('fsdp')
- grad_shrink_bias: float32 [1280], P('fsdp')
Inputs may be any that keep to these rules, and one draw needn't show every extreme that they name: `lengths`: in every micro-batch some clip has all 1024 positions valid.
All inputs are finite; a program needn't handle non-finite values.
Results may differ from a plain program's by a relative error of at most 0.014.
Values may be sent and summed in bfloat16 or wider, within the bound.
A program may use at most 512 MiB of HBM per device.

v0:
```python
from functools import partial
from types import SimpleNamespace

import jax
import jax.numpy as jnp
from jax import lax
from jax.experimental import pallas as pl
from jax.experimental.pallas import tpu as pltpu
from jax.sharding import PartitionSpec as P

H = 16
HD = 80
CHIPS = 4
CORES = 2
DEV_CLIP = CHIPS * CORES
OWN_HEADS = H // CHIPS
OWN_FEATURES = OWN_HEADS * HD
QKV_WIDTH = 1024
TILE = 256
ROW_GAIN_ONE, ROW_SHIFT_ONE, ROW_GAIN_TWO, ROW_SHIFT_TWO, ROW_BIAS_OUT, ROW_BIAS_SHRINK = range(6)

EPS = 1e-05
NEG = -1000000000.0
SCALE = HD ** (-0.5)
BF = jnp.bfloat16
F32 = jnp.float32


def dot_nn(left, right):
    return lax.dot_general(left, right, (((1,), (0,)), ((), ())), preferred_element_type=F32)


def dot_nt(left, right):
    return lax.dot_general(left, right, (((1,), (1,)), ((), ())), preferred_element_type=F32)


def dot_tn(left, right):
    return lax.dot_general(left, right, (((0,), (0,)), ((), ())), preferred_element_type=F32)


def norm_parts(rows):
    mean = jnp.mean(rows, -1, keepdims=True)
    centered = rows - mean
    inverse = lax.rsqrt(jnp.mean(centered * centered, -1, keepdims=True) + EPS)
    return centered * inverse, inverse


def norm_backward(gradient, normed, inverse, gain):
    scaled = gradient * gain
    return inverse * (
        scaled
        - jnp.mean(scaled, -1, keepdims=True)
        - normed * jnp.mean(scaled * normed, -1, keepdims=True)
    )


def place(device):
    return device // DEV_CLIP, (device % DEV_CLIP) // CORES, device % CORES


def flipped(number, by):
    low, high = number % 2, number // 2
    if by & 1:
        low = 1 - low
    if by & 2:
        high = 1 - high
    return high * 2 + low


SEND_SEMS, RECV_SEMS, LOCAL_SEMS = 104, 217, 18


def block_kernel(fused, planes, micro, tok, width, ff_own, share, ff_share, *refs):
    names = ["x", "dy", "lengths"]
    if fused:
        names += ["av", "bv", "cv_", "dv", "ev", "fv"] + ["expand_bias", "query_bias", "value_bias", "wq", "wk", "wv", "we", "wo", "ws"]
    else:
        names += ["vec", "wq", "we", "wo", "ws"]
    names += ["bo", "ig", "vo", "vt", "gq", "ge", "go", "gs"]
    if fused:
        names += ["Lq", "Le", "Lo", "Ls"]
    names += ["Wq", "We", "Wo", "Ws", "xg", "dyg", "a2g", "drg", "act", "dhid"]
    names += ["q", "kv", "mixed", "lse", "dmix", "dq", "dl"]
    names += ["sb", "sbo", "rb", "rbo", "resid", "dresid", "vfin", "be", "bq", "vexp", "vqkv", "vrow"]
    if fused:
        names += ["so", "oo", "ao", "aq", "ae", "alq", "ale", "cv", "cp"]
        names += [letter + end for letter in "ut" for end in ("0", "1", "2", "z", "p", "s")]
        names += ["ready_e", "ready_s", "ready_q"]
    names += ["ssem", "rsem", "lsem"]
    r = SimpleNamespace(**dict(zip(names, refs, strict=True)))
    if fused:
        r.vectors = (r.av, r.bv, r.cv_, r.dv, r.ev, r.fv)
    r.dqkv = r.dhid.at[:, :, 0:QKV_WIDTH]
    me = lax.axis_index("fsdp")
    c, k, e = place(me)
    rows = CHIPS * tok

    def chip_peer(by):
        return c * DEV_CLIP + flipped(k, by) * CORES + e

    sibling = c * DEV_CLIP + k * CORES + (1 - e)

    def plane_peer(by):
        return flipped(c, by) * DEV_CLIP + k * CORES + e

    counters = SimpleNamespace(remote=0, local=0, sends=0, free=[])
    pending = []

    def send_semaphore():
        if counters.free:
            return counters.free.pop()
        counters.sends += 1
        return counters.sends - 1

    def flush(count=None):
        for wait in pending[:len(pending) - (count or 0)]:
            wait()

    def send(src, dst, device):
        i = counters.remote
        counters.remote += 1
        out = send_semaphore()
        copy = pltpu.make_async_remote_copy(
            src_ref=src, dst_ref=dst, send_sem=r.ssem.at[out], recv_sem=r.rsem.at[i],
            device_id=(device,), device_id_type=pl.DeviceIdType.MESH,
        )
        copy.start()
        state = SimpleNamespace(sent=False)

        def wait_send():
            if not state.sent:
                state.sent = True
                counters.free.append(out)
                copy.wait_send()

        copy_handle = (copy.wait_recv, wait_send)
        pending.append(wait_send)
        return copy_handle

    def send_if(held, src, dst, device, due, arriving):
        i = counters.remote
        counters.remote += 1
        out = send_semaphore()

        def copy(source, target, to):
            return pltpu.make_async_remote_copy(
                src_ref=source, dst_ref=target, send_sem=r.ssem.at[out], recv_sem=r.rsem.at[i],
                device_id=(to,), device_id_type=pl.DeviceIdType.MESH,
            )

        @pl.when(held)
        def _():
            copy(src(), dst(), device).start()

        state = SimpleNamespace(sent=False)

        def wait_send():
            if not state.sent:
                state.sent = True
                counters.free.append(out)

                @pl.when(held)
                def _():
                    copy(src(), dst(), device).wait_send()

        def wait_recv():
            @pl.when(due)
            def _():
                copy(arriving(), arriving(), sibling).wait_recv()

        copy_handle = (wait_recv, wait_send)
        pending.append(wait_send)
        return copy_handle

    def line_group(mine, theirs):
        return SimpleNamespace(mine=mine, theirs=theirs, steps=[], swaps=[])

    def forward(group, step):
        mine, theirs = group.mine, group.theirs
        if step > 0:
            recv_all(group.steps[step - 1])
        if step < planes - 1:
            n = step + 1
            group.steps.append([
                send_if(
                    (c >= n - 1) & (c < planes - 1), lambda: mine(c - n + 1), lambda: mine(c - n + 1),
                    me + DEV_CLIP, c >= n, lambda: mine(c - n),
                ),
                send_if(
                    (c + n - 1 < planes) & (c >= 1), lambda: mine(c + n - 1), lambda: mine(c + n - 1),
                    me - DEV_CLIP, c + n < planes, lambda: mine(c + n),
                ),
            ])
        if step == 0:
            group.swaps.append(send(mine(c), theirs(c), sibling))
        else:
            for held, i in ((c >= step, c - step), (c + step < planes, c + step)):
                group.swaps.append(
                    send_if(
                        held, lambda i=i: mine(i), lambda i=i: theirs(i), sibling, held, lambda i=i: theirs(i)
                    )
                )

    def group_sent(group):
        sent_all(sum(group.steps, []) + group.swaps)

    def local(src, dst):
        i = counters.local
        counters.local += 1
        copy = pltpu.make_async_copy(src, dst, r.lsem.at[i])
        copy.start()
        return copy.wait

    def recv_all(handles):
        for handle in handles:
            handle[0]()

    def sent_all(handles):
        for handle in handles:
            handle[1]()

    Wq, We, Wo, Ws = r.Wq, r.We, r.Wo, r.Ws
    Ws2 = Ws.reshape(ff_own, width)

    def flat(ref):
        return ref.reshape(micro * rows, width)

    chip_rows = CHIPS * share
    plane_rows = CORES * chip_rows
    chip_halves = (slice(0, chip_rows // 2), slice(chip_rows // 2, chip_rows))

    def stacked(ref, count, lanes):
        return flat(ref).at[0:count * chip_rows].reshape(count, chip_rows, width).at[:, :, 0:lanes]

    def by_core(own, other):
        return jnp.where(e == 0, own, other), jnp.where(e == 0, other, own)

    def join_rows(own, other, count):
        first, second = by_core(own, other)
        pieces = []
        for j in range(count):
            pieces += [first[j * share:(j + 1) * share], second[j * share:(j + 1) * share]]
        return jnp.concatenate(pieces, 0)

    def split_rows(block, count):
        pieces = [block[j * share:(j + 1) * share] for j in range(2 * count)]
        return by_core(jnp.concatenate(pieces[0::2], 0), jnp.concatenate(pieces[1::2], 0))

    def join_planes(own, other, out):
        @pl.loop(0, planes)
        def _(i):
            block = join_rows(own[i].astype(F32), other[i].astype(F32), CHIPS)
            out[pl.ds(pl.multiple_of(i * plane_rows, plane_rows), plane_rows), :] = block.astype(BF)

    def split_planes(grads, own, other):
        @pl.loop(0, planes)
        def _(i):
            block = grads[pl.ds(pl.multiple_of(i * plane_rows, plane_rows), plane_rows), :].astype(F32)
            mine, theirs = split_rows(block, CHIPS)
            own[i] = mine.astype(BF)
            other[i] = theirs.astype(BF)

    k_x, k_y, k_far = flipped(k, 1), flipped(k, 2), flipped(k, 3)
    x_peer, y_peer, far_peer = chip_peer(1), chip_peer(2), chip_peer(3)
    top, low = slice(0, tok // 2), slice(tok // 2, tok)

    def gather_start(src, dst, b):
        return [dst.at[b], [send(src, dst.at[b, k], x_peer), send(src, dst.at[b, k], y_peer)]]

    def gather_relay(gather):
        dst, handles = gather
        handles[0][0]()
        handles.append(send(dst.at[k_x, top], dst.at[k_x, top], y_peer))
        handles[1][0]()
        handles.append(send(dst.at[k_y, low], dst.at[k_y, low], x_peer))

    def gather_finish(gather):
        recv_all(gather[1][2:])

    def reduce_start(slots, landing, b):
        slots, landing = slots.at[b], landing.at[b]
        return [slots, landing, [
            send(slots.at[k_far, top], landing.at[2, top], x_peer),
            send(slots.at[k_far, low], landing.at[2, low], y_peer),
            send(slots.at[k_x, top], landing.at[0, top], x_peer),
            send(slots.at[k_y, low], landing.at[1, low], y_peer),
        ]]

    def reduce_relay(reduction):
        slots, landing, handles = reduction
        handles[0][0]()
        slots[k_y, top] = (slots[k_y, top].astype(F32) + landing[2, top].astype(F32)).astype(BF)
        handles.append(send(slots.at[k_y, top], landing.at[1, top], y_peer))
        handles[1][0]()
        slots[k_x, low] = (slots[k_x, low].astype(F32) + landing[2, low].astype(F32)).astype(BF)
        handles.append(send(slots.at[k_x, low], landing.at[0, low], x_peer))

    def reduce_finish(reduction):
        slots, landing, handles = reduction
        recv_all(handles[2:])
        return slots[k].astype(F32) + landing[0].astype(F32) + landing[1].astype(F32)

    sb, sbo, rb, rbo = r.sb, r.sbo, r.rb, r.rbo
    vfin = r.vfin

    def vec_row(index):
        return vfin[index:index + 1, :]

    def add_row(index, value):
        r.vrow[index:index + 1, :] += value

    def norm_one(b):
        x_local[b]()
        gather_finish(x_gather[b])
        sent_all(x_gather[b][1])

        @pl.loop(0, CHIPS)
        def _(i):
            normed, _inverse = norm_parts(r.xg[b, i].astype(F32))
            r.xg[b, i] = (normed * vec_row(ROW_GAIN_ONE) + vec_row(ROW_SHIFT_ONE)).astype(BF)

    a1_rows = r.xg.reshape(micro, rows, width)
    a2_rows = r.a2g.reshape(micro, rows, width)
    dy_rows = r.dyg.reshape(micro, rows, width)
    dr_rows = r.drg.reshape(micro, rows, width)
    half = rows // 2

    def project(b):
        @pl.loop(0, 2)
        def _(i):
            at = pl.ds(pl.multiple_of(i * half, half), half)
            out = (dot_nn(a1_rows[b, at, :], Wq[...]) + r.bq[...]).astype(BF)
            for h in range(OWN_HEADS):
                r.q[b, h, at, :] = out[:, h * HD:(h + 1) * HD]
                for part in range(2):
                    low = (part + 1) * OWN_FEATURES + h * HD
                    r.kv[b, part, h, e, at, :] = out[:, low:low + HD]

        return [send(r.kv.at[b, :, :, e], r.kv.at[b, :, :, e], sibling)]

    keys = CORES * rows
    chunk_places = [(2 * (i % CHIPS) + i // CHIPS) * tok for i in range(DEV_CLIP)]

    def masked_scores(b, key_rows, query_rows):
        raw = dot_nt(key_rows, query_rows)
        index = lax.broadcasted_iota(jnp.int32, (tok, raw.shape[1]), 0)
        length = r.lengths[b, c]
        return jnp.concatenate(
            [
                raw[i * tok:(i + 1) * tok] * SCALE
                if first + tok <= keys // 2
                else jnp.where(index < length - first, raw[i * tok:(i + 1) * tok] * SCALE, NEG)
                for i, first in enumerate(chunk_places)
            ],
            0,
        )

    def attend(b, start, stop):
        @pl.loop(start, stop)
        def _(step):
            h, part = step // 2, step % 2
            at = pl.ds(pl.multiple_of(part * half, half), half)
            key_rows = r.kv[b, 0, h].reshape(keys, HD)
            value_rows = r.kv[b, 1, h].reshape(keys, HD)
            scores = masked_scores(b, key_rows, r.q[b, h, at, :])
            peak = jnp.max(scores, 0, keepdims=True)
            exponent = jnp.exp(scores - peak)
            sums = jnp.sum(exponent, 0, keepdims=True)
            probs = (exponent * (1.0 / sums)).astype(BF)
            r.lse[b, h, :, at] = peak + jnp.log(sums)
            r.mixed[b, h, :, at] = dot_tn(value_rows, probs).astype(BF)

    def tiles(start, stop, body):
        @pl.loop(start, stop)
        def _(i):
            body(pl.ds(pl.multiple_of(i * TILE, TILE), TILE))

    def partial_sum(slots, b, product):
        view = slots.reshape(micro, rows, width)

        def body(at):
            view[b, :, at] = product(at).astype(BF)

        tiles(0, width // TILE, body)

    mixed = r.mixed.reshape(micro, OWN_FEATURES, rows)

    def mix_out(b):
        partial_sum(sb, b, lambda at: dot_tn(mixed[b], Wo[:, at]))
        return reduce_start(sb, rb, b)

    def norm_two(b, reduction):
        residual = r.x[b].astype(F32) + reduce_finish(reduction) + vec_row(ROW_BIAS_OUT)
        r.resid[b] = residual
        normed, _inverse = norm_parts(residual)
        r.a2g[b, k] = (normed * vec_row(ROW_GAIN_TWO) + vec_row(ROW_SHIFT_TWO)).astype(BF)
        return gather_start(r.a2g.at[b, k], r.a2g, b)

    def feed(b, start, stop):
        def body(at):
            hidden = dot_nn(a2_rows[b], We[:, at]) + r.be[:, at]
            grad_active = dot_nt(dy_rows[b], Ws2[at, :]).astype(BF).astype(F32)
            normal = 0.5 * (1.0 + lax.erf(hidden * 0.7071067811865476))
            r.act[b, :, at] = (hidden * normal).astype(BF)
            density = jnp.exp(-0.5 * hidden * hidden) * 0.3989422804014327
            grad_hidden = (grad_active * (normal + hidden * density)).astype(BF)
            r.dhid[b, :, at] = grad_hidden
            r.vexp[:, at] += jnp.sum(grad_hidden.astype(F32), 0, keepdims=True)

        tiles(start, stop, body)

    def hidden_back(b, earlier):
        sent_all(earlier[2])
        partial_sum(sb, b, lambda at: dot_nt(r.dhid[b], We[at, :]))
        return reduce_start(sb, rb, b)

    def finish_hidden(b, reduction):
        gradient = reduce_finish(reduction)
        normed, inverse = norm_parts(r.resid[b])
        dy_own = r.dy[b].astype(F32)
        total = dy_own + norm_backward(gradient, normed, inverse, vec_row(ROW_GAIN_TWO))
        r.dresid[b] = total
        r.drg[b, k] = total.astype(BF)
        gather = gather_start(r.drg.at[b, k], r.drg, b)
        add_row(ROW_GAIN_TWO, jnp.sum(gradient * normed, 0, keepdims=True))
        add_row(ROW_SHIFT_TWO, jnp.sum(gradient, 0, keepdims=True))
        add_row(ROW_BIAS_OUT, jnp.sum(total, 0, keepdims=True))
        add_row(ROW_BIAS_SHRINK, jnp.sum(dy_own, 0, keepdims=True))
        return gather

    def weight_gradient(count, lefts, rights, out):
        def body(at):
            total = dot_tn(lefts[0, :, at], rights[0])
            for b in range(1, micro):
                total = total + dot_tn(lefts[b, :, at], rights[b])
            out[at, :] = total.astype(BF)

        tiles(0, count // TILE, body)

    def mixed_gradient(b):
        @pl.loop(0, 2)
        def _(i):
            at = pl.ds(pl.multiple_of(i * half, half), half)
            out = dot_nt(dr_rows[b, at, :], Wo[...]).astype(BF)
            for h in range(OWN_HEADS):
                r.dmix[h, at, :] = out[:, h * HD:(h + 1) * HD]

    def attend_back(b, start, stop):
        @pl.loop(start, stop)
        def _(h):
            key_rows = r.kv[b, 0, h].reshape(keys, HD)
            value_rows = r.kv[b, 1, h].reshape(keys, HD)
            grad_keys = None
            grad_values = None
            for part in range(2):
                at = pl.ds(part * half, half)
                query_rows = r.q[b, h, at, :]
                mix_rows = r.dmix[h, at, :]
                probs = jnp.exp(masked_scores(b, key_rows, query_rows) - r.lse[b, h, :, at])
                grad_probs = dot_nt(value_rows, mix_rows)
                inner = jnp.sum(probs * grad_probs, 0, keepdims=True)
                grad_scores = (probs * (grad_probs - inner)).astype(BF)
                grad_query = dot_tn(key_rows, grad_scores) * SCALE
                r.dq[h, at, :] = grad_query.T.astype(BF)
                key_term = dot_nn(grad_scores, query_rows)
                value_term = dot_nn(probs.astype(BF), mix_rows)
                grad_keys = key_term if grad_keys is None else grad_keys + key_term
                grad_values = value_term if grad_values is None else grad_values + value_term
            r.kv[b, 0, h] = (grad_keys * SCALE).astype(BF).reshape(CORES, rows, HD)
            r.kv[b, 1, h] = grad_values.astype(BF).reshape(CORES, rows, HD)

    def swap_back(b, start, stop):
        return [send(r.kv.at[b, :, start:stop, 1 - e], r.dl.at[b, :, start:stop], sibling)]

    def join_gradients(b, handles):
        recv_all(handles)

        @pl.loop(0, CHIPS)
        def _(i):
            at = pl.ds(pl.multiple_of(i * tok, tok), tok)
            pieces = [r.dq[h, at, :] for h in range(OWN_HEADS)]
            for part in range(2):
                for h in range(OWN_HEADS):
                    pair = r.kv[b, part, h, e, at, :].astype(F32) + r.dl[b, part, h, at, :].astype(F32)
                    pieces.append(pair.astype(BF))
            pieces.append(jnp.zeros((tok, QKV_WIDTH - 3 * OWN_FEATURES), BF))
            line = jnp.concatenate(pieces, 1)
            r.dqkv[b, at, :] = line
            r.vqkv[...] += jnp.sum(line.astype(F32), 0, keepdims=True)

    def input_start(b, earlier):
        sent_all(earlier[2])
        partial_sum(sb, b, lambda at: dot_nt(r.dqkv[b], Wq[at, :]))
        return reduce_start(sb, rb, b)

    def finish_input(b, reduction):
        gradient = reduce_finish(reduction)
        normed, inverse = norm_parts(r.x[b].astype(F32))
        back = norm_backward(gradient, normed, inverse, vec_row(ROW_GAIN_ONE))
        r.ig[b] = (r.dresid[b] + back).astype(BF)
        add_row(ROW_GAIN_ONE, jnp.sum(gradient * normed, 0, keepdims=True))
        add_row(ROW_SHIFT_ONE, jnp.sum(gradient, 0, keepdims=True))

    def finish_out(b, reduction):
        total = r.resid[b] + reduce_finish(reduction) + vec_row(ROW_BIAS_SHRINK)
        r.bo[b] = total.astype(BF)

    def sum_group(space, slots):
        return SimpleNamespace(space=space, slots=slots, right={}, left={})

    def add_passing(group, hops):
        space, slots = group.space, group.slots
        for side, held, i, slot in (
            (group.right, (c >= 1) & (c - 1 + hops < planes), c - 1 + hops, hops - 1),
            (group.left, (c <= planes - 2) & (c + 1 - hops >= 0), c + 1 - hops, 5 - hops),
        ):
            side[hops][0]()

            @pl.when(held)
            def _():
                space[i] = (space[i].astype(F32) + slots[slot][...].astype(F32)).astype(BF)

    def sum_step(group, hops):
        space, slots = group.space, group.slots
        if hops < planes - 1:
            add_passing(group, hops + 1)
        group.right[hops] = send_if(
            c + hops < planes, lambda: space.at[c + hops], lambda: slots[hops - 1], me + DEV_CLIP,
            (c >= 1) & (c - 1 + hops < planes), lambda: slots[hops - 1],
        )
        group.left[hops] = send_if(
            c - hops >= 0, lambda: space.at[c - hops], lambda: slots[5 - hops], me - DEV_CLIP,
            (c <= planes - 2) & (c + 1 - hops >= 0), lambda: slots[5 - hops],
        )

    def sum_finish(group, out):
        space, slots = group.space, group.slots
        out(space[c].astype(F32), False)
        for side, held, slot in ((group.right, c >= 1, 0), (group.left, c <= planes - 2, 4)):
            side[1][0]()

            @pl.when(held)
            def _():
                out(slots[slot][...].astype(F32), True)

    def to_blocks(ref, first):
        def put(total, more):
            for j in range(total.shape[0] // share):
                piece = total[j * share:(j + 1) * share]
                ref[first + j] = ref[first + j] + piece if more else piece

        return put

    def to_rows(ref):
        def put(total, more):
            ref[...] = ref[...] + total if more else total

        return put

    def sibling_add(handles, landing, fetched, out, mine):
        recv_all(handles)
        sent_all(handles)
        local(landing, fetched)()

        @pl.loop(0, planes)
        def _(i):
            out[i] = (mine(i).astype(F32) + fetched[i].astype(F32)).astype(BF)

    def free_slots(ready):
        for side, held, device in ((0, c >= 1, me - DEV_CLIP), (1, c <= planes - 2, me + DEV_CLIP)):

            @pl.when(held)
            def _():
                pl.semaphore_signal(
                    ready.at[1 - side], inc=1, device_id=(device,), device_id_type=pl.DeviceIdType.MESH
                )

    def await_slots(ready):
        for side, held in ((0, c >= 1), (1, c <= planes - 2)):

            @pl.when(held)
            def _():
                pl.semaphore_wait(ready.at[side], 1)

    resid, dresid = r.resid, r.dresid
    x_local = [local(r.x.at[b], r.xg.at[b, k]) for b in range(micro)]
    dy_local = [local(r.dy.at[b], r.dyg.at[b, k]) for b in range(micro)]
    x_gather = [None] * micro
    dy_gather = [None] * micro
    if fused:
        expand = [dresid.at[0, 0:share], dresid.at[0, share:2 * share], dresid.at[0, 2 * share:3 * share], dresid.at[1, 0:share]]
        first_rows = tok - share
        loads = [local(ref, resid.at[0, i * share:(i + 1) * share]) for i, ref in enumerate((r.wq, r.wk, r.wv))]
        loads.append(local(r.wo, resid.at[1, 0:share]))
        expand_loads = [local(r.we.at[:, i * width:(i + 1) * width], expand[i]) for i in range(planes)]
        expand_loads.append(local(r.ws.at[0:first_rows], resid.at[1, share:tok]))
        expand_loads.append(local(r.ws.at[first_rows:ff_share], dresid.at[1, share:ff_share - first_rows + share]))
        peers = [chip_peer(by) for by in (1, 2, 3)] + [sibling]
        if fused:
            peers += [plane_peer(by) for by in range(1, planes)]
        barrier = pltpu.get_barrier_semaphore()
        for peer in peers:
            pl.semaphore_signal(barrier, inc=1, device_id=(peer,), device_id_type=pl.DeviceIdType.MESH)
        for load in loads:
            load()
        matrices = [resid[0, i * share:(i + 1) * share] for i in range(3)]
        for j in range(CHIPS):
            pieces = [
                matrix[:, (i * CHIPS + j) * HD:(i * CHIPS + j + 1) * HD] for matrix in matrices for i in range(planes)
            ]
            pieces.append(jnp.zeros((share, QKV_WIDTH - 3 * OWN_FEATURES), F32))
            r.aq[j] = jnp.concatenate(pieces, 1).astype(BF)
        r.so[c] = resid[1, 0:share].astype(BF)
        compact = jnp.concatenate([jnp.pad(ref[...], ((0, 0), (0, 256 - share))) for ref in r.vectors], 0)
        tail = jnp.pad(r.expand_bias[...], ((0, 0), (0, 256 - ff_share)))
        pair = [jnp.pad(ref[...], ((0, 0), (0, 128 - share))) for ref in (r.query_bias, r.value_bias)]
        r.cv[c] = jnp.concatenate([compact, tail, jnp.concatenate(pair, 1)], 0)
        pl.semaphore_wait(barrier, len(peers))
        wq_mine, wq_other = stacked(r.drg, planes, QKV_WIDTH), stacked(r.a2g, planes, QKV_WIDTH)
        we_mine, we_other = stacked(r.act, planes, ff_own), stacked(r.dhid, planes, ff_own)
        lines_q = [
            line_group(lambda i, at=at: wq_mine.at[i, at], lambda i, at=at: wq_other.at[i, at]) for at in chip_halves
        ]
        line_e = line_group(lambda i: we_mine.at[i], lambda i: we_other.at[i])
        line_o = line_group(lambda i: r.so.at[i], lambda i: r.oo.at[i])
        line_s = line_group(lambda i: Ws.at[i, e], lambda i: Ws.at[i, e])

        def pack_plane(blocks, out):
            out[c] = jnp.concatenate([blocks[j].astype(F32) for j in range(CHIPS)], 0).astype(BF)

        wq_plane = [send(r.aq.at[flipped(k, by)], r.alq.at[k], chip_peer(by)) for by in (3, 1, 2)]
        vec_z = [send(r.cv.at[c], r.cv.at[c], plane_peer(by)) for by in range(1, planes)]
        forward(line_o, 0)
        r.alq[k] = r.aq[k]
        recv_all(vec_z)
        r.cp[e, k] = r.cv[...]
        vec_p = [send(r.cv, r.cp.at[e, k], chip_peer(by)) for by in (1, 2, 3)]
        x_gather[0] = gather_start(r.x.at[0], r.xg, 0)
        recv_all(wq_plane)
        pack_plane(r.alq, wq_mine)
        for line in lines_q:
            forward(line, 0)
        for load in expand_loads:
            load()
        ff_part = width // planes
        for j in range(CHIPS):
            pieces = [block[:, j * ff_part:(j + 1) * ff_part] for block in expand]
            r.ae[j] = jnp.concatenate(pieces, 1).astype(BF)
        we_plane = [send(r.ae.at[flipped(k, by)], r.ale.at[k], chip_peer(by)) for by in (3, 1, 2)]
        r.ale[k] = r.ae[k]
        rows_s = [resid[1, share:tok], dresid[1, share:ff_share - first_rows + share]]
        Ws[c, e] = jnp.concatenate(rows_s, 0).astype(BF)
        recv_all(vec_p)
        vec_s = [send(r.cp.at[e], r.cp.at[e], sibling)]
        recv_all(vec_s)
        places = [(i, f) for i in range(planes) for f in range(CORES)]
        vfin[...] = jnp.concatenate(
            [r.cp[f, j, i][:, 0:share] for i in range(planes) for j in range(CHIPS) for f in range(CORES)], 1
        )
        r.be[...] = jnp.concatenate([r.cp[f, k, i][6:7, 0:ff_share] for i, f in places], 1)
        bias = [jnp.concatenate([r.cp[f, k, i][7:8, at:at + share] for i, f in places], 1) for at in (0, 128)]
        blank = jnp.zeros((1, OWN_FEATURES), F32)
        r.bq[...] = jnp.concatenate([bias[0], blank, bias[1], blank[:, :QKV_WIDTH - 3 * OWN_FEATURES]], 1)
        gather_relay(x_gather[0])
        x_gather[1] = gather_start(r.x.at[1], r.xg, 1)
        forward(line_o, 1)
        for line in lines_q:
            forward(line, 1)
        recv_all(we_plane)
        pack_plane(r.ale, we_mine)
    else:
        peers = [chip_peer(by) for by in (1, 2, 3)] + [sibling]
        if fused:
            peers += [plane_peer(by) for by in range(1, planes)]
        barrier = pltpu.get_barrier_semaphore()
        for peer in peers:
            pl.semaphore_signal(barrier, inc=1, device_id=(peer,), device_id_type=pl.DeviceIdType.MESH)
        pl.semaphore_wait(barrier, len(peers))
        loads = [local(r.wq, Wq), local(r.we, We), local(r.wo, Wo), local(r.ws, Ws2)]
        for b in range(micro):
            x_gather[b] = gather_start(r.x.at[b], r.xg, b)
        vfin[...] = r.vec[...]
        r.be[...] = r.vec[6:7, :]
        r.bq[...] = r.vec[7:8, :QKV_WIDTH]
        gather_relay(x_gather[0])
        for load in loads:
            load()
    for ref in (r.vrow, r.vexp, r.vqkv):
        ref[...] = jnp.zeros_like(ref)
    norm_one(0)
    if fused:
        forward(line_o, 2)
        for line in lines_q:
            forward(line, 2)
        forward(line_e, 0)
        forward(line_s, 0)
    gather_relay(x_gather[1])
    dy_gather[0] = gather_start(r.dy.at[0], r.dyg, 0)
    norm_one(1)
    if fused:
        forward(line_o, 3)
        for line in lines_q:
            forward(line, 3)
        for line in lines_q:
            recv_all(line.swaps)
        join_planes(wq_mine, wq_other, Wq)
    kv_swap = [None] * micro
    kv_swap[0] = project(0)
    gather_relay(dy_gather[0])
    dy_gather[1] = gather_start(r.dy.at[1], r.dyg, 1)
    kv_swap[1] = project(1)
    recv_all(kv_swap[0])
    attend(0, 0, OWN_HEADS)
    if fused:
        forward(line_e, 1)
    attend(0, OWN_HEADS, 2 * OWN_HEADS)
    if fused:
        recv_all(line_o.swaps)
        for i in range(planes):
            pair = join_rows(r.so[i].astype(F32), r.oo[i].astype(F32), 1)
            Wo[i * HD:(i + 1) * HD, :] = pair.astype(BF)
    mix_reduce = [mix_out(0), None]
    gather_relay(dy_gather[1])
    recv_all(kv_swap[1])
    attend(1, 0, OWN_HEADS)
    if fused:
        forward(line_s, 1)
    attend(1, OWN_HEADS, 2 * OWN_HEADS - 1)
    reduce_relay(mix_reduce[0])
    attend(1, 2 * OWN_HEADS - 1, 2 * OWN_HEADS)
    mix_reduce[1] = mix_out(1)
    if fused:
        forward(line_e, 2)
    second_gather = [norm_two(0, mix_reduce[0]), None]
    if fused:
        forward(line_s, 2)
    reduce_relay(mix_reduce[1])
    gather_relay(second_gather[0])
    second_gather[1] = norm_two(1, mix_reduce[1])
    if fused:
        forward(line_e, 3)
        recv_all(line_e.swaps)
        group_sent(line_e)
        for line in lines_q:
            group_sent(line)
        join_planes(we_mine, we_other, We)
    gather_finish(second_gather[0])
    dy_local[0]()
    gather_finish(dy_gather[0])
    if fused:
        forward(line_s, 3)
        recv_all(line_s.swaps)
    flush(20)
    feed(0, 0, 3)
    gather_relay(second_gather[1])
    feed(0, 3, ff_own // TILE)
    hidden_reduce = [hidden_back(0, mix_reduce[0]), None]
    gather_finish(second_gather[1])
    dy_local[1]()
    gather_finish(dy_gather[1])
    feed(1, 0, ff_own // TILE)
    reduce_relay(hidden_reduce[0])
    hidden_reduce[1] = hidden_back(1, mix_reduce[1])
    weight_gradient(width, a2_rows, r.dhid, We)
    resid_gather = [finish_hidden(0, hidden_reduce[0]), None]
    if fused:
        sent_all(wq_plane + we_plane)
        group_sent(line_o)
        group_sent(line_s)
        sent_all(second_gather[0][1] + second_gather[1][1])
        free_slots(r.ready_e)
        parts_e = We.reshape(planes, 2, chip_rows, ff_own)
        split_planes(We, parts_e.at[:, 0], parts_e.at[:, 1])
        ge_s = [send(parts_e.at[:, 1], r.Le, sibling)]
    partial_sum(sbo, 0, lambda at: dot_nn(r.act[0], Ws2[:, at]))
    if fused:
        sum_e = sum_group(parts_e.at[:, 0], [flat(r.a2g).at[i * chip_rows:(i + 1) * chip_rows] for i in range(5)])
        sibling_add(ge_s, r.Le, parts_e.at[:, 1], parts_e.at[:, 0], lambda i: parts_e[i, 0])
        await_slots(r.ready_e)
        sum_step(sum_e, 3)
    partial_sum(sbo, 1, lambda at: dot_nn(r.act[1], Ws2[:, at]))
    reduce_relay(hidden_reduce[1])
    weight_gradient(ff_own, r.act, dy_rows, Ws2)
    if fused:
        sent_all(dy_gather[0][1] + dy_gather[1][1])
        free_slots(r.ready_s)
        gs_s = [send(Ws.at[:, 1 - e], r.Ls, sibling)]
    gather_relay(resid_gather[0])
    if fused:
        places_s = [flat(r.a2g).at[5 * ff_share:6 * ff_share]]
        for ref in (r.dyg, r.act):
            places_s += [flat(ref).at[i * ff_share:(i + 1) * ff_share] for i in (4, 5)]
        sum_s = sum_group(Ws.at[:, e], places_s)
        sibling_add(gs_s, r.Ls, Ws.at[:, 1 - e], Ws.at[:, e], lambda i: Ws[i, e])
        await_slots(r.ready_s)
        sum_step(sum_s, 3)
    resid_gather[1] = finish_hidden(1, hidden_reduce[1])
    if fused:
        sum_step(sum_e, 2)
    flush(20)
    gather_finish(resid_gather[0])
    mixed_gradient(0)
    sent_all(kv_swap[0] + kv_swap[1])
    attend_back(0, 0, 2)
    gather_relay(resid_gather[1])
    out_reduce = [reduce_start(sbo, rbo, 0), None]
    if fused:
        sum_step(sum_s, 2)
    attend_back(0, 2, OWN_HEADS)
    swap = swap_back(0, 0, OWN_HEADS)
    gather_finish(resid_gather[1])
    mixed_gradient(1)
    lead = dot_nn(mixed[0], dr_rows[0])
    for other in range(1, micro):
        lead = lead + dot_nn(mixed[other], dr_rows[other])
    if fused:
        space_o, other_o = r.so, r.oo
        for i in range(planes):
            mine, theirs = split_rows(lead[i * HD:(i + 1) * HD], 1)
            space_o[i] = mine.astype(BF)
            other_o[i] = theirs.astype(BF)
        go_s = [send(other_o, r.Lo, sibling)]
    else:
        Wo[...] = lead.astype(BF)
    join_gradients(0, swap)
    input_reduce = [input_start(0, hidden_reduce[0]), None]
    if fused:
        sum_step(sum_e, 1)
    attend_back(1, 0, 2)
    last_swap = swap_back(1, 0, 2)
    reduce_relay(out_reduce[0])
    if fused:
        sum_o = sum_group(space_o, [r.ao.at[i] for i in range(5)])
        sibling_add(go_s, r.Lo, other_o, space_o, lambda i: space_o[i])
        sum_step(sum_s, 1)
        sum_step(sum_o, 3)
    attend_back(1, 2, OWN_HEADS)
    last_swap += swap_back(1, 2, OWN_HEADS)
    reduce_relay(input_reduce[0])
    join_gradients(1, last_swap)
    input_reduce[1] = input_start(1, hidden_reduce[1])
    weight_gradient(width, a1_rows, r.dqkv, Wq)
    flush(20)
    if fused:
        free_slots(r.ready_q)
        parts_q = Wq.reshape(planes, 2, chip_rows, QKV_WIDTH)
        split_planes(Wq, parts_q.at[:, 0], parts_q.at[:, 1])
        gq_s = [send(parts_q.at[:, 1], r.Lq, sibling)]
        sum_step(sum_o, 2)
        five = stacked(r.dhid, 5, QKV_WIDTH)
        sums_q = [sum_group(parts_q.at[:, 0, at], [five.at[i, at] for i in range(5)]) for at in chip_halves]
    finish_input(0, input_reduce[0])
    if fused:
        sibling_add(gq_s, r.Lq, parts_q.at[:, 1], parts_q.at[:, 0], lambda i: parts_q[i, 0])
        await_slots(r.ready_q)
        for group in sums_q:
            sum_step(group, 3)
    def vector_step(group, step, last):
        zero, one, two, from_z, from_plane, from_core = group
        if step == 0:
            return [send(zero, from_core, sibling)]
        if step == 1:
            one[...] = zero[...] + from_core[...]
            return [send(one, from_z.at[by - 1], plane_peer(by)) for by in range(1, planes)]
        if step == 2:
            total = one[...]
            for by in range(1, planes):
                total = total + from_z[by - 1]
            two[...] = total
            return [send(two, from_plane.at[by - 1], chip_peer(by)) for by in (1, 2, 3)]
        others = from_plane[0] + from_plane[1] + from_plane[2]
        shared = lax.broadcasted_iota(jnp.int32, others.shape, 0) < 6
        last[...] = two[...] + jnp.where(shared, others, 0.0)

    if fused:
        group_u = (r.u0, r.u1, r.u2, r.uz, r.up, r.us)
        group_t = (r.t0, r.t1, r.t2, r.tz, r.tp, r.ts)
    padded = jnp.concatenate([r.vqkv[...], jnp.zeros((1, width - QKV_WIDTH), F32)], 1)
    early = jnp.concatenate([r.vrow[0:6, :], r.vexp[...], padded], 0)
    if fused:
        r.u0[...] = early
        moved = vector_step(group_u, 0, None)
    reduce_relay(input_reduce[1])
    out_reduce[1] = reduce_start(sbo, rbo, 1)
    finish_out(0, out_reduce[0])
    if fused:
        recv_all(moved)
        moved = vector_step(group_u, 1, None)
        sum_finish(sum_s, to_rows(r.gs))
        sum_finish(sum_e, to_blocks(r.ge, 0))
        for j in range(CHIPS):
            r.ae[j] = r.ge[j].astype(BF)
        sum_step(sum_o, 1)
    if fused:
        ge_p = [send(r.ae.at[flipped(k, by)], r.ale.at[k], chip_peer(by)) for by in (3, 1, 2)]
        recv_all(moved)
        moved = vector_step(group_u, 2, None)
        for group in sums_q:
            sum_step(group, 2)
    finish_input(1, input_reduce[1])
    late = r.vrow[0:2, :]
    if fused:
        r.t0[...] = late
        moved_late = vector_step(group_t, 0, None)
    reduce_relay(out_reduce[1])
    if fused:
        recv_all(moved)
        vector_step(group_u, 3, r.vo)
        recv_all(ge_p)
        for by in (1, 2, 3):
            r.ge[flipped(k, by)] = r.ale[flipped(k, by)].astype(F32)
        recv_all(moved_late)
        moved_late = vector_step(group_t, 1, None)
        for group in sums_q:
            sum_step(group, 1)
        recv_all(moved_late)
        moved_late = vector_step(group_t, 2, None)
        sum_finish(sum_o, to_rows(r.go))
        recv_all(moved_late)
        vector_step(group_t, 3, r.vt)
    finish_out(1, out_reduce[1])
    if fused:
        for i, group in enumerate(sums_q):
            sum_finish(group, to_blocks(r.gq, i * CHIPS // 2))
        for j in range(CHIPS):
            r.aq[j] = r.gq[j].astype(BF)
        gq_p = [send(r.aq.at[flipped(k, by)], r.alq.at[k], chip_peer(by)) for by in (3, 1, 2)]
        recv_all(gq_p)
        for by in (1, 2, 3):
            r.gq[flipped(k, by)] = r.alq[flipped(k, by)].astype(F32)
    else:
        r.vo[...] = early
        r.vt[...] = late
        stores = [local(Wq, r.gq), local(We, r.ge), local(Wo, r.go), local(Ws2, r.gs)]
        for store in stores:
            store()
    flush()


def run_block(fused, planes, x, dy, lengths, vectors, weights_in, share, ff_share):
    micro, tok, width = x.shape
    ff_own = width
    rows = CHIPS * tok
    vmem = pl.BlockSpec(memory_space=pltpu.VMEM)
    anywhere = pl.BlockSpec(memory_space=pl.ANY)
    smem = pl.BlockSpec(memory_space=pltpu.SMEM)

    def shape(*dims, dtype=BF):
        return jax.ShapeDtypeStruct(dims, dtype)

    outs = [
        (shape(micro, tok, width), vmem),
        (shape(micro, tok, width), vmem),
        (shape(8, width, dtype=F32), vmem),
        (shape(2, width, dtype=F32), vmem),
    ]
    if fused:
        outs += [
            (shape(CHIPS, share, QKV_WIDTH, dtype=F32), vmem),
            (shape(CHIPS, share, ff_own, dtype=F32), vmem),
            (shape(share, width, dtype=F32), vmem),
            (shape(ff_share, width, dtype=F32), vmem),
        ]
        outs += [
            (shape(planes, CHIPS * share, QKV_WIDTH), anywhere),
            (shape(planes, CHIPS * share, ff_own), anywhere),
            (shape(planes, share, width), anywhere),
            (shape(planes, ff_share, width), anywhere),
        ]
    else:
        outs += [
            (shape(width, QKV_WIDTH), anywhere),
            (shape(width, ff_own), anywhere),
            (shape(OWN_FEATURES, width), anywhere),
            (shape(ff_own, width), anywhere),
        ]
    if fused:
        weights = [
            pltpu.VMEM((width, QKV_WIDTH), BF),
            pltpu.VMEM((width, ff_own), BF),
            pltpu.VMEM((OWN_FEATURES, width), BF),
            pltpu.VMEM((planes, CORES, ff_share, width), BF),
        ]
    else:
        weights = [
            pltpu.VMEM((width, QKV_WIDTH), BF),
            pltpu.VMEM((width, ff_own), BF),
            pltpu.VMEM((OWN_FEATURES, width), BF),
            pltpu.VMEM((ff_own, width), BF),
        ]
    scratch = weights + [
        pltpu.VMEM((micro, CHIPS, tok, width), BF),
        pltpu.VMEM((micro, CHIPS, tok, width), BF),
        pltpu.VMEM((micro, CHIPS, tok, width), BF),
        pltpu.VMEM((micro, CHIPS, tok, width), BF),
        pltpu.VMEM((micro, rows, ff_own), BF),
        pltpu.VMEM((micro, rows, ff_own), BF),
        pltpu.VMEM((micro, OWN_HEADS, rows, HD), BF),
        pltpu.VMEM((micro, 2, OWN_HEADS, CORES, rows, HD), BF),
        pltpu.VMEM((micro, OWN_HEADS, HD, rows), BF),
        pltpu.VMEM((micro, OWN_HEADS, 1, rows), F32),
        pltpu.VMEM((OWN_HEADS, rows, HD), BF),
        pltpu.VMEM((OWN_HEADS, rows, HD), BF),
        pltpu.VMEM((micro, 2, OWN_HEADS, rows, HD), BF),
        pltpu.VMEM((micro, CHIPS, tok, width), BF),
        pltpu.VMEM((micro, CHIPS, tok, width), BF),
        pltpu.VMEM((micro, CHIPS - 1, tok, width), BF),
        pltpu.VMEM((micro, CHIPS - 1, tok, width), BF),
        pltpu.VMEM((micro, tok, width), F32),
        pltpu.VMEM((micro, tok, width), F32),
        pltpu.VMEM((8, width), F32),
        pltpu.VMEM((1, ff_own), F32),
        pltpu.VMEM((1, QKV_WIDTH), F32),
        pltpu.VMEM((1, ff_own), F32),
        pltpu.VMEM((1, QKV_WIDTH), F32),
        pltpu.VMEM((8, width), F32),
    ]
    if fused:
        scratch += [
            pltpu.VMEM((planes, share, width), BF),
            pltpu.VMEM((planes, share, width), BF),
            pltpu.VMEM((5, share, width), BF),
            pltpu.VMEM((CHIPS, share, QKV_WIDTH), BF),
            pltpu.VMEM((CHIPS, share, ff_own), BF),
            pltpu.VMEM((CHIPS, share, QKV_WIDTH), BF),
            pltpu.VMEM((CHIPS, share, ff_own), BF),
        ]
        scratch += [
            pltpu.VMEM((planes, 8, 256), F32),
            pltpu.VMEM((CORES, CHIPS, planes, 8, 256), F32),
        ]
        for lines in (8, 2):
            scratch += [pltpu.VMEM((lines, width), F32) for _ in range(3)]
            scratch += [pltpu.VMEM((planes - 1, lines, width), F32), pltpu.VMEM((CHIPS - 1, lines, width), F32)]
            scratch.append(pltpu.VMEM((lines, width), F32))
        scratch += [pltpu.SemaphoreType.REGULAR((2,)) for _ in range(3)]
    scratch += [
        pltpu.SemaphoreType.DMA((SEND_SEMS,)),
        pltpu.SemaphoreType.DMA((RECV_SEMS,)),
        pltpu.SemaphoreType.DMA((LOCAL_SEMS,)),
    ]
    return pl.pallas_call(
        partial(block_kernel, fused, planes, micro, tok, width, ff_own, share, ff_share),
        out_shape=[out for out, _ in outs],
        in_specs=[vmem, vmem, smem] + [vmem] * len(vectors) + [anywhere] * len(weights_in),
        out_specs=[spec for _, spec in outs],
        scratch_shapes=scratch,
        compiler_params=pltpu.CompilerParams(
            collective_id=0, has_side_effects=True, vmem_limit_bytes=63 * 1000 * 1000
        ),
    )(x, dy, lengths, *vectors, *weights_in)


def finish_kernel(planes, share, ff_share, bo, ig, vo, vt, gq, ge, go, gs, *refs):
    device = lax.axis_index("fsdp")
    c, _, e = place(device)
    outs, (blocks_q, blocks_e, lines, last_lines, sems) = refs[:17], refs[17:]
    moves = [(vo, lines), (vt, last_lines), (gq, blocks_q), (ge, blocks_e)]
    moves += [(bo, outs[0]), (ig, outs[1]), (go, outs[6]), (gs, outs[7])]
    copies = [pltpu.make_async_copy(src, dst, sems.at[i]) for i, (src, dst) in enumerate(moves)]
    for copy in copies:
        copy.start()
    for copy in copies[:4]:
        copy.wait()
    part = ge.shape[2] // planes
    for n in range(planes):
        for j in range(CHIPS):
            at = (n * CHIPS + j) * part
            outs[5][:, at:at + part] = blocks_e[j][:, n * part:(n + 1) * part]
    for i, out in enumerate(outs[2:5]):
        first = i * OWN_FEATURES
        out[...] = jnp.concatenate(
            [blocks_q[j][:, first + n * HD:first + (n + 1) * HD] for n in range(planes) for j in range(CHIPS)], 1
        )
    vo, vt = lines, last_lines
    width = vo.shape[1]

    def own(lines, start, size):
        lane = lax.broadcasted_iota(jnp.int32, (width, size), 0)
        pick = (lane == start + lax.broadcasted_iota(jnp.int32, (width, size), 1)).astype(F32)
        return lax.dot_general(
            lines, pick, (((1,), (0,)), ((), ())), precision=lax.Precision.HIGHEST, preferred_element_type=F32
        )

    early, late = own(vo[...], device * share, share), own(vt[...], device * share, share)
    expand = own(vo[...], (2 * c + e) * ff_share, ff_share)
    query = own(vo[...], (2 * c + e) * share, share)
    value = own(vo[...], 2 * OWN_FEATURES + (2 * c + e) * share, share)
    for out, line in zip(
        outs[8:],
        [late[0:1], late[1:2]] + [early[i:i + 1] for i in range(2, 6)] + [expand[6:7], query[7:8], value[7:8]],
        strict=True,
    ):
        out[...] = line
    for copy in copies[4:]:
        copy.wait()


def finish_block(planes, share, ff_share, results):
    shapes = [results[0], results[1]] + [jax.ShapeDtypeStruct((share, results[2].shape[1]), F32)] * 3
    shapes += [jax.ShapeDtypeStruct((share, CHIPS * results[5].shape[2]), F32), results[6], results[7]]
    shapes = [jax.ShapeDtypeStruct(s.shape, s.dtype) for s in shapes]
    shapes += [jax.ShapeDtypeStruct((1, share), F32)] * 6
    shapes += [jax.ShapeDtypeStruct((1, size), F32) for size in (ff_share, share, share)]
    vmem = pl.BlockSpec(memory_space=pltpu.VMEM)
    anywhere = pl.BlockSpec(memory_space=pl.ANY)
    held = [results[4], results[5], results[2], results[3]]
    return pl.pallas_call(
        partial(finish_kernel, planes, share, ff_share),
        out_shape=shapes,
        in_specs=[anywhere] * 8,
        out_specs=[vmem] * 17,
        scratch_shapes=[pltpu.VMEM(a.shape, a.dtype) for a in held] + [pltpu.SemaphoreType.DMA((8,))],
        compiler_params=pltpu.CompilerParams(vmem_limit_bytes=60 * 1000 * 1000),
    )(*results)


def by_chip(matrix, part):
    rows = matrix.shape[0]
    return matrix.reshape(rows, -1, CHIPS, part).transpose(2, 0, 1, 3).reshape(CHIPS, rows, -1)


def from_chips(blocks, part):
    rows = blocks.shape[1]
    return blocks.reshape(CHIPS, rows, -1, part).transpose(1, 2, 0, 3).reshape(rows, -1)


def body(
    inputs, cotangent, lengths, first_gain, first_shift, query_weight, query_bias, key_weight,
    value_weight, value_bias, output_weight, output_bias, second_gain, second_shift,
    expand_weight, expand_bias, shrink_weight, shrink_bias,
):
    device = lax.axis_index("fsdp")
    count = lax.axis_size("fsdp")
    c, k, e = place(device)
    planes = count // DEV_CLIP
    width = inputs.shape[2]
    share = query_weight.shape[0]
    ff_share = shrink_weight.shape[0]
    ff_part = width // 4
    fused = planes == 4 and share * 2 == HD and ff_share * 2 == ff_part
    plain = (first_gain, first_shift, second_gain, second_shift, output_bias, shrink_bias)
    matrices = (query_weight, key_weight, value_weight, expand_weight, output_weight, shrink_weight)
    if fused:
        vectors = [v.reshape(1, -1) for v in plain + (expand_bias, query_bias, value_bias)]
        got = run_block(True, planes, inputs, cotangent, lengths, vectors, matrices, share, ff_share)
        done = finish_block(planes, share, ff_share, got[:8])
        block_out, input_grad, grad_query_w, grad_key_w, grad_value_w, grad_expand_w, grad_output_w, grad_shrink_w = done[:8]
        owned = [line[0] for line in done[8:14]]
        grad_expand_b, grad_query_b, grad_value_b = (line[0] for line in done[14:])
    else:

        def whole(array):
            return lax.all_gather(array, "fsdp", axis=0, tiled=True)

        def mine(blocks):
            return lax.dynamic_index_in_dim(blocks, k, 0, keepdims=False)

        full = [whole(w.astype(BF)) for w in matrices]
        pieces = [mine(by_chip(w, HD)) for w in full[:3]]
        pieces.append(jnp.zeros((width, QKV_WIDTH - 3 * OWN_FEATURES), BF))
        wq = jnp.concatenate(pieces, 1)
        we = mine(by_chip(full[3], ff_part))
        wo = mine(by_chip(full[4].T, HD)).T
        ws = mine(by_chip(full[5].T, ff_part)).T
        bias_e = mine(by_chip(whole(expand_bias)[None], ff_part))
        bias_q = mine(by_chip(whole(query_bias)[None], HD))
        bias_v = mine(by_chip(whole(value_bias)[None], HD))
        blank = jnp.zeros((1, width - 3 * OWN_FEATURES), F32)
        bias_row = jnp.concatenate([bias_q, jnp.zeros_like(bias_q), bias_v, blank], 1)
        vec = jnp.concatenate([jnp.stack([whole(v) for v in plain]), bias_e, bias_row])
        got = run_block(False, planes, inputs, cotangent, lengths, (vec,), (wq, we, wo, ws), share, ff_share)
        block_out, input_grad, sums, late, gq, ge, go, gs = got[:8]

        def spread(block, part):
            places = lax.broadcasted_iota(jnp.int32, (CHIPS, 1, 1), 0) == k
            return from_chips(jnp.where(places, block.astype(F32)[None], 0.0), part)

        def owned_sum(array):
            return lax.psum_scatter(array, "fsdp", scatter_dimension=0, tiled=True)

        grad_query_w, grad_key_w, grad_value_w = (
            owned_sum(spread(gq[:, i * OWN_FEATURES:(i + 1) * OWN_FEATURES], HD)) for i in range(3)
        )
        grad_expand_w = owned_sum(spread(ge, ff_part))
        grad_output_w = owned_sum(spread(go.T, HD).T)
        grad_shrink_w = owned_sum(spread(gs.T, ff_part).T)
        owned = [owned_sum(late[i]) for i in range(2)] + [owned_sum(sums[i]) for i in range(2, len(plain))]
        line_q, line_v = sums[7:8, :OWN_FEATURES], sums[7:8, 2 * OWN_FEATURES:3 * OWN_FEATURES]
        grad_expand_b = owned_sum(spread(sums[6:7], ff_part)[0])
        grad_query_b = owned_sum(spread(line_q, HD)[0])
        grad_value_b = owned_sum(spread(line_v, HD)[0])
    return (
        block_out,
        input_grad,
        owned[0],
        owned[1],
        grad_query_w,
        grad_query_b,
        grad_key_w,
        grad_value_w,
        grad_value_b,
        grad_output_w,
        owned[4],
        owned[2],
        owned[3],
        grad_expand_w,
        grad_expand_b,
        grad_shrink_w,
        owned[5],
    )


def solution(mesh):
    rows, matrix, vector = P(None, "fsdp", None), P("fsdp", None), P("fsdp")
    in_specs = (
        rows, rows, P(), vector, vector, matrix, vector, matrix, matrix, vector, matrix, vector,
        vector, vector, matrix, vector, matrix, vector,
    )
    out_specs = (
        rows, rows, vector, vector, matrix, vector, matrix, matrix, vector, matrix, vector,
        vector, vector, matrix, vector, matrix, vector,
    )
    return jax.shard_map(body, mesh=mesh, in_specs=in_specs, out_specs=out_specs, check_vma=False)
```

profile of v0, /device:TPU:0, one launch (start us, length us, event | category | flops | bytes accessed | tf_op | source)
XLA Modules:
  0.0 233.7 jit_solution(15583327646834191288)
XLA Ops:
  0.7 227.5 %shard_map.305 = (bf16[2,128,1280]{2,1,0:T(8,128)(2,1)}, bf16[2,128,1280]{2,1,0:T(8,128)(2,1)}, f32[8,1280]{1,0:T(8,128)}, f32[2,1280]{1,0:T(2,128)}, f32[4,40,1...) custom-call(bf16[2,128,1280]{2,1,0:T(8,128)(2,1)} %refs_0_.1, ...), custom_call_target="tpu_custom_call" | custom-call | tf_op jit(solution)/shard_map/pallas_call | solution.py:1042
  228.1 5.4 %shard_map.306 = (bf16[2,128,1280]{2,1,0:T(8,128)(2,1)}, bf16[2,128,1280]{2,1,0:T(8,128)(2,1)}, f32[40,1280]{1,0:T(8,128)}, f32[40,1280]{1,0:T(8,128)}, f32[40,1...) custom-call(bf16[2,128,1280]{2,1,0:T(8,128)(2,1)} %get-tuple-element, ...), custom_call_target="tpu_custom_call" | custom-call | tf_op jit(solution)/shard_map/pallas_call | solution.py:1108
where the time goes:
time: 234 us
  Pallas kernels  233 us (100%)
    pallas_call x1, Pallas kernels, run_block(): pl.pallas_call(partial(block_kernel, fused, planes, micro, tok, width, ff...  227 us
    pallas_call x1, Pallas kernels, finish_block(): pl.pallas_call(partial(finish_kernel, planes, share, ff_share), out_shape...  5.41 us

commit v1 on v0

--- a/solution.py
+++ b/solution.py
@@ -1076,13 +1076,10 @@
     width = vo.shape[1]
 
     def own(lines, start, size):
-        lane = lax.broadcasted_iota(jnp.int32, (width, size), 0)
-        pick = (lane == start + lax.broadcasted_iota(jnp.int32, (width, size), 1)).astype(F32)
-        return lax.dot_general(
-            lines, pick, (((1,), (0,)), ((), ())), precision=lax.Precision.HIGHEST, preferred_element_type=F32
-        )
-
-    early, late = own(vo[...], device * share, share), own(vt[...], device * share, share)
+        return pltpu.roll(lines, lax.rem(width - start, width), 1)[:, 0:size]
+
+    early = own(vo[...], device * share, share)
+    late = own(jnp.concatenate([vt[...], vo[2:8, :]], 0), device * share, share)
     expand = own(vo[...], (2 * c + e) * ff_share, ff_share)
     query = own(vo[...], (2 * c + e) * share, share)
     value = own(vo[...], 2 * OWN_FEATURES + (2 * c + e) * share, share)

time: 234 us -> 233 us (level)
  no operation moved by 1% of the time
where the time goes in v1:
time: 233 us; the launch traced here: 232 us
  Pallas kernels  232 us (100%)
    pallas_call x1, Pallas kernels, run_block(): pl.pallas_call(partial(block_kernel, fused, planes, micro, tok, width, ff...  227 us

profile of v1, /device:TPU:0, one launch (start us, length us, event | category | flops | bytes accessed | tf_op | source)
XLA Modules:
  0.0 232.4 jit_solution(7536000073265747149)
XLA Ops:
  0.7 227.5 %shard_map.305 = (bf16[2,128,1280]{2,1,0:T(8,128)(2,1)}, bf16[2,128,1280]{2,1,0:T(8,128)(2,1)}, f32[8,1280]{1,0:T(8,128)}, f32[2,1280]{1,0:T(2,128)}, f32[4,40,1...) custom-call(bf16[2,128,1280]{2,1,0:T(8,128)(2,1)} %refs_0_.1, ...), custom_call_target="tpu_custom_call" | custom-call | tf_op jit(solution)/shard_map/pallas_call | solution.py:1042
  228.1 4.1 %shard_map.306 = (bf16[2,128,1280]{2,1,0:T(8,128)(2,1)}, bf16[2,128,1280]{2,1,0:T(8,128)(2,1)}, f32[40,1280]{1,0:T(8,128)}, f32[40,1280]{1,0:T(8,128)}, f32[40,1...) custom-call(bf16[2,128,1280]{2,1,0:T(8,128)(2,1)} %get-tuple-element, ...), custom_call_target="tpu_custom_call" | custom-call | tf_op jit(solution)/shard_map/pallas_call | solution.py:1105

commit v2 on v1

--- a/solution.py
+++ b/solution.py
@@ -751,9 +751,9 @@
         forward(line_s, 3)
         recv_all(line_s.swaps)
     flush(20)
-    feed(0, 0, 3)
+    feed(0, 0, 4)
     gather_relay(second_gather[1])
-    feed(0, 3, ff_own // TILE)
+    feed(0, 4, ff_own // TILE)
     hidden_reduce = [hidden_back(0, mix_reduce[0]), None]
     gather_finish(second_gather[1])
     dy_local[1]()

time: 233 us -> 232 us (level)
  no operation moved by 1% of the time
where the time goes in v2:
time: 232 us
  Pallas kernels  231 us (100%)
    pallas_call x1, Pallas kernels, run_block(): pl.pallas_call(partial(block_kernel, fused, planes, micro, tok, width, ff...  227 us

profile of v2, /device:TPU:0, one launch (start us, length us, event | category | flops | bytes accessed | tf_op | source)
XLA Modules:
  0.0 232.2 jit_solution(9271656339246827877)
XLA Ops:
  0.7 227.2 %shard_map.305 = (bf16[2,128,1280]{2,1,0:T(8,128)(2,1)}, bf16[2,128,1280]{2,1,0:T(8,128)(2,1)}, f32[8,1280]{1,0:T(8,128)}, f32[2,1280]{1,0:T(2,128)}, f32[4,40,1...) custom-call(bf16[2,128,1280]{2,1,0:T(8,128)(2,1)} %refs_0_.1, ...), custom_call_target="tpu_custom_call" | custom-call | tf_op jit(solution)/shard_map/pallas_call | solution.py:1042
  227.9 4.1 %shard_map.306 = (bf16[2,128,1280]{2,1,0:T(8,128)(2,1)}, bf16[2,128,1280]{2,1,0:T(8,128)(2,1)}, f32[40,1280]{1,0:T(8,128)}, f32[40,1280]{1,0:T(8,128)}, f32[40,1...) custom-call(bf16[2,128,1280]{2,1,0:T(8,128)(2,1)} %get-tuple-element, ...), custom_call_target="tpu_custom_call" | custom-call | tf_op jit(solution)/shard_map/pallas_call | solution.py:1105
